TPU v7x, 32 devices: a whole 2x2x4 slice. The times are simulated.
32 devices in a mesh: groups: 2 (over x), space: 16 (over z, y, core).
Axes of the slice: x: 2, y: 2, z: 4, core: 2. Of those that a mesh axis runs over, the one named last changes fastest.
Arguments:
- snapshots: bfloat16 [256, 128, 128], P(('groups', 'space')), parts along dimension 0, may hold values from -6 to 6
- weights: bfloat16 [256, 128, 1024], P(('groups', 'space')), parts along dimension 0, may hold values from -6 to 6
- neighbours: int32 [256, 8], P(('groups', 'space')), parts along dimension 0, may hold values from 0 to 127, as said below
- time_of: int32 [256], P('groups'), parts along dimension 0, may hold values from 0 to 127, each once
Outputs:
- new_weights: float32 [256, 128, 1024], P(('groups', 'space')), parts along dimension 0
- cell_error: float32 [256, 128], P(('groups', 'space')), parts along dimension 0
There are 2 independent parts, one for each index of `groups`. A program takes and returns all parts, laid end to end along the dimension named above; each array names one. Nothing has to cross between parts.
Inputs may be any that keep to these rules, and one draw needn't show every extreme that they name: `neighbours`: row g lists 8 groups in a drawn order: g itself, g - 4, g + 4, and 5 more within 4 groups of g, all counted cyclically modulo 128; entries may repeat. `time_of`: each time index appears once.
All inputs are finite; a program needn't handle non-finite values.
Results may differ from a plain program's by a relative error of at most 0.002.
Values may be sent and summed in bfloat16 or wider, within the bound.
A program may use at most 64 MiB of HBM per device.

v0:
```python
import jax
import jax.numpy as jnp
from jax import lax
from jax.sharding import PartitionSpec as P

HALO = 4


def extended(x, sides, width):
    for axis, dim in sides:
        size, length = (lax.axis_size(axis), x.shape[dim])
        up = [(i, (i + 1) % size) for i in range(size)]
        down = [(j, i) for i, j in up]
        last = lax.slice_in_dim(x, length - width, length, axis=dim)
        initial = lax.slice_in_dim(x, 0, width, axis=dim)
        before = lax.ppermute(last, axis, up)
        after = lax.ppermute(initial, axis, down)
        x = jnp.concatenate([before, x, after], axis=dim)
    return x


def shards(snapshots, weights, neighbours, time_of):
    step_rate = 100.0
    g_dev = weights.shape[0]
    width = weights.shape[1]
    span = weights.shape[2]
    n_dev = lax.axis_size("space")
    total = time_of.shape[0]
    owned = lax.all_to_all(snapshots, "space", split_axis=1, concat_axis=0, tiled=True)
    padded = extended(owned, (("space", 1),), HALO)
    order = jnp.argsort(time_of)
    ordered = padded[order]
    target = jnp.roll(ordered[:, HALO : HALO + g_dev], -1, 0)
    first = lax.axis_index("space") * g_dev
    all_groups = g_dev * n_dev
    here = jnp.arange(g_dev, dtype=jnp.int32)
    local = (neighbours - (first + here)[:, None] + HALO) % all_groups + here[:, None]
    scale = 1.0 / jnp.sqrt(jnp.float32(span))
    rows_step = min(total, 256)
    turns = total // rows_step

    def block_rows(turn):
        rows = lax.dynamic_slice_in_dim(ordered, turn * rows_step, rows_step, 0)
        goal = lax.dynamic_slice_in_dim(target, turn * rows_step, rows_step, 0).astype(jnp.float32)
        inputs = rows[:, local].reshape(rows_step, g_dev, span)
        live = (turn * rows_step + jnp.arange(rows_step) < total - 1).astype(jnp.float32)[
            :, None, None
        ]
        return (inputs, goal, live)

    def add_grad(turn, grad):
        inputs, goal, live = block_rows(turn)
        pred = (
            jnp.einsum("tgc,goc->tgo", inputs, weights, preferred_element_type=jnp.float32) * scale
        )
        resid = ((pred - goal) * live).astype(jnp.bfloat16)
        return grad + jnp.einsum("tgo,tgc->goc", resid, inputs, preferred_element_type=jnp.float32)

    grad = lax.fori_loop(0, turns, add_grad, jnp.zeros((g_dev, width, span), jnp.float32))
    new_weights = weights.astype(jnp.float32) - step_rate * (grad * (2.0 * scale / (total - 1)))
    new_rounded = new_weights.astype(jnp.bfloat16)

    def add_error(turn, error):
        inputs, goal, live = block_rows(turn)
        after = (
            jnp.einsum("tgc,goc->tgo", inputs, new_rounded, preferred_element_type=jnp.float32)
            * scale
            - goal
        ) * live
        return error + jnp.sum(after * after, axis=0)

    error = lax.fori_loop(0, turns, add_error, jnp.zeros((g_dev, width), jnp.float32))
    return (new_weights, error / (total - 1))


def solution(mesh):
    return jax.shard_map(
        shards,
        mesh=mesh,
        in_specs=(
            P(("groups", "space"), None, None),
            P(("groups", "space"), None, None),
            P(("groups", "space"), None),
            P("groups"),
        ),
        out_specs=(P(("groups", "space"), None, None), P(("groups", "space"), None)),
        check_vma=False,
    )
```

profile of v0, /device:TPU:0, one launch (start us, length us, event | category | flops | bytes accessed | tf_op | source)
XLA Modules:
  0.0 38.4 jit_solution(6387515284216943299)
XLA Ops:
  0.6 1.8 %copy.21 = bf16[8,128,128]{2,0,1:T(8,128)(2,1)} copy(bf16[8,128,128]{2,1,0:T(8,128)(2,1)} %param.4) | data formatting | bytes 524288 | tf_op args[0]
  2.5 7.4 %all-to-all-start = ((bf16[8,128,128]{2,0,1:T(8,128)(2,1)}), bf16[8,128,128]{2,0,1:T(8,128)(2,1)S(1)}, u32[]{:S(2)}, u32[]{:S(2)}) async-start(bf16[8,128,128]{2,0,1:T(8,128)(2,1)} %copy.21), calls=%async_computation | async-start | bytes 524288 | tf_op jit(solution)/shard_map/all_to_all | solution.py:29
  9.9 3.2 %sort.17 = (s32[128]{0:T(128)}, s32[128]{0:T(128)S(1)}) sort(s32[128]{0:T(128)} %param.7, s32[128]{0:T(128)S(1)} %iota.22), dimensions={0}, to_apply=%region_0.0 | sort | flops 896 | bytes 2048 | tf_op jit(solution)/shard_map/jit(argsort)/sort | solution.py:31
  13.1 0.8 %compare_select_fusion = s32[8,8]{1,0:T(8,128)S(1)} fusion(s32[8,8]{1,0:T(8,128)} %param.6, s32[8]{0:T(128)S(1)} %iota_add_fusion), kind=kLoop, calls=%fused_computation.28 | loop fusion | flops 1088 | bytes 544 | tf_op jit(solution)/shard_map/while/body/eval_jaxpr/select_n | solution.py:45
  13.8 6.1 %all-to-all-done = bf16[8,128,128]{2,0,1:T(8,128)(2,1)S(1)} async-done(((bf16[8,128,128]{2,0,1:T(8,128)(2,1)}), bf16[8,128,128]{2,0,1:T(8,128)(2,1)S(1)}, u32[]{:S(2)}, u32[]{:S(2)}) %all-to-all-start) | async-done | bytes 262176 | tf_op jit(solution)/shard_map/all_to_all | solution.py:29
  19.9 0.1 fusion.63
  20.0 0.1 collective-permute-start
  20.1 4.4 %collective-permute-start.1 = (bf16[128,4,128]{2,1,0:T(4,128)(2,1)S(1)}, bf16[128,4,128]{2,1,0:T(4,128)(2,1)S(1)}, u32[]{:S(2)}, u32[]{:S(2)}) collective-permute-start(bf16[128,4,128]{2,1,0:T(4,128)(2,1)S(1)} %get-tuple-element.33), channel_id=1, source_target_pairs={{1,0},{2,1},{3,2},{4,3},{5,4},{6,5},{7,6},{8,7},{9,8},{10,9},{11,1... | collective-permute-start | bytes 393224 | tf_op jit(solution)/shard_map/ppermute | solution.py:17
  24.5 0.1 reshape.30
  24.6 2.6 %collective-permute-done = bf16[128,4,128]{2,1,0:T(4,128)(2,1)S(1)} collective-permute-done((bf16[128,4,128]{2,1,0:T(4,128)(2,1)S(1)}, bf16[128,4,128]{2,1,0:T(4,128)(2,1)S(1)}, u32[]{:S(2)}, u32[]{:S(2)}) %collective-permute-start) | collective-permute-done | bytes 131104 | tf_op jit(solution)/shard_map/ppermute | solution.py:16
  27.2 0.0 collective-permute-done.1
  27.2 0.3 pad_maximum_fusion
  27.5 0.7 %gather_fusion = bf16[128,16,128]{2,1,0:T(8,128)(2,1)S(1)} fusion(bf16[128,16,128]{2,1,0:T(8,128)(2,1)S(1)} %pad_maximum_fusion, s32[1024]{0:T(1024)S(1)} %pad_clamp_fusion.1), kind=kCustom, calls=%fused_computation | custom fusion | bytes 1049088 | tf_op jit(solution)/shard_map/gather | solution.py:32
  28.2 0.1 copy.24
  28.4 0.1 slice.27
  28.4 1.0 %gather_fusion.1 = bf16[64,128,128]{2,1,0:T(8,128)(2,1)S(1)} fusion(bf16[128,16,128]{2,0,1:T(8,128)(2,1)S(1)} %copy.24, s32[1024]{0:T(1024)S(1)} %pad_clamp_fusion), kind=kCustom, calls=%fused_computation.1 | custom fusion | bytes 4194560 | tf_op jit(solution)/shard_map/while/body/eval_jaxpr/gather | solution.py:45
  29.4 5.5 %multiply_subtract_fusion = f32[8,128,1024]{2,1,0:T(8,128)} fusion(bf16[8,128,1024]{2,1,0:T(8,128)(2,1)} %param.5, bf16[8,8,16,8,128]{4,3,2,1,0:T(8,128)(2,1)S(1)} %bitcast.60, f32[128]{0:T(128)S(1)} %compare_convert_fusion, bf16[1,8,128]{2,0,1:T(2,128)(2,1)S(1)} %slice.28, bf16[127,8,128]{2,0,1:T(8,128)(2,1)S(1)} %slice.27), kind=kOutput, calls=%fused_computation.2 | convolution fusion | flops 541065216 | bytes 8651264 | tf_op jit(solution)/shard_map/while/body/eval_jaxpr/tgo,tgc->goc/dot_general | solution.py:57
  34.9 2.9 %fusion.51 = f32[8,128]{1,0:T(8,128)S(1)} fusion(bf16[8,8,16,8,128]{4,3,2,1,0:T(8,128)(2,1)S(1)} %bitcast.61, f32[8,128,1024]{2,1,0:T(8,128)} %multiply_subtract_fusion, f32[128]{0:T(128)S(1)} %compare_convert_fusion, bf16[1,8,128]{2,0,1:T(2,128)(2,1)S(1)} %slice.28, bf16[127,8,128]{2,0,1:T(8,128)(2,1)S(1)} %slice.27), kind=kOutput, calls=%fused_computation.22 | convolution fusion | flops 270662656 | bytes 6558208 | tf_op jit(solution)/shard_map/while/body/eval_jaxpr/tgc,goc->tgo/dot_general | solution.py:66
  37.8 0.6 %broadcast_multiply_fusion = f32[8,128]{1,0:T(8,128)} fusion(f32[8,128]{1,0:T(8,128)S(1)} %fusion.51), kind=kLoop, calls=%fused_computation.37 | loop fusion | flops 1024 | bytes 8192 | tf_op jit(solution)/shard_map/div | solution.py:73
  (8 shorter events, 0.1 us)
Async XLA Ops:
  2.5 17.4 %all-to-all-start = ((bf16[8,128,128]{2,0,1:T(8,128)(2,1)}), bf16[8,128,128]{2,0,1:T(8,128)(2,1)S(1)}, u32[]{:S(2)}, u32[]{:S(2)}) async-start(bf16[8,128,128]{2,0,1:T(8,128)(2,1)} %copy.21), calls=%async_computation | async-start | bytes 524288 | tf_op jit(solution)/shard_map/all_to_all | solution.py:29
  20.0 7.1 %collective-permute-start = (bf16[128,4,128]{2,1,0:T(4,128)(2,1)S(1)}, bf16[128,4,128]{2,1,0:T(4,128)(2,1)S(1)}, u32[]{:S(2)}, u32[]{:S(2)}) collective-permute-start(bf16[128,4,128]{2,1,0:T(4,128)(2,1)S(1)} %get-tuple-element.32), channel_id=1, source_target_pairs={{0,1},{1,2},{2,3},{3,4},{4,5},{5,6},{6,7},{7,8},{8,9},{9,10},{10,1... | collective-permute-start | bytes 393224 | tf_op jit(solution)/shard_map/ppermute | solution.py:16
  20.1 7.1 %collective-permute-start.1 = (bf16[128,4,128]{2,1,0:T(4,128)(2,1)S(1)}, bf16[128,4,128]{2,1,0:T(4,128)(2,1)S(1)}, u32[]{:S(2)}, u32[]{:S(2)}) collective-permute-start(bf16[128,4,128]{2,1,0:T(4,128)(2,1)S(1)} %get-tuple-element.33), channel_id=1, source_target_pairs={{1,0},{2,1},{3,2},{4,3},{5,4},{6,5},{7,6},{8,7},{9,8},{10,9},{11,1... | collective-permute-start | bytes 393224 | tf_op jit(solution)/shard_map/ppermute | solution.py:17
where the time goes:
time: 38.7 us; the launch traced here: 38.4 us
  starting transfers between devices  11.9 us (31%)
  waiting for transfers between devices  8.62 us (22%)
  matrix products  8.4 us (22%)
  other arithmetic  4.87 us (13%)
  local copies, waits for them, and re-layouts  3.91 us (10%)
  between operations  0.72 us (2%)
    all_to_all x1, starting transfers between devices, shards(): lax.all_to_all(snapshots, 'space', split_axis=1, concat_axis=0, tiled=True)  7.39 us
    all_to_all x1, waiting for transfers between devices, shards(): lax.all_to_all(snapshots, 'space', split_axis=1, concat_axis=0, tiled=True)  6.06 us
    dot_general x1, matrix products, add_grad(): jnp.einsum('tgo,tgc->goc', resid, inputs, preferred_element_type=jnp.floa...  5.49 us
    ppermute x1, starting transfers between devices, extended(): after = lax.ppermute(initial, axis, down)  4.43 us
    sort x1, other arithmetic, shards(): order = jnp.argsort(time_of)  3.19 us
    dot_general x1, matrix products, add_error(): jnp.einsum('tgc,goc->tgo', inputs, new_rounded, preferred_element_type=jn...  2.91 us
    ppermute x1, waiting for transfers between devices, extended(): before = lax.ppermute(last, axis, up)  2.55 us
    unnamed x1, local copies, waits for them, and re-layouts  1.83 us
  transfers between devices with their start and end apart: 3, of which 2 were waited for; matrix products, arithmetic and copies ran while one was open for 11% of the time, Pallas kernels for 0%

commit v1 on v0

--- a/solution.py
+++ b/solution.py
@@ -26,7 +26,12 @@
     span = weights.shape[2]
     n_dev = lax.axis_size("space")
     total = time_of.shape[0]
-    owned = lax.all_to_all(snapshots, "space", split_axis=1, concat_axis=0, tiled=True)
+    owned = jnp.concatenate(
+        lax.all_to_all(
+            jnp.stack(jnp.split(snapshots, lax.axis_size("space"), axis=1)), "space", 0, 0
+        ),
+        axis=0,
+    )
     padded = extended(owned, (("space", 1),), HALO)
     order = jnp.argsort(time_of)
     ordered = padded[order]

time: 38.7 us -> 58.8 us (1.52); the launches traced: 38.4 us -> 57.7 us
  local copies, waits for them, and re-layouts: 3.91 us -> 23.2 us
    unnamed x1 -> x15, local copies, waits for them, and re-layouts: 1.83 us -> 19.9 us
    another operation x0 -> x1, local copies, waits for them, and re-layouts: none -> 1.32 us  [shards(): jnp.stack(jnp.split(snapshots, lax.axis_size('space'), axis=1))]
  transfers between devices with their start and end apart: 3 -> 3, of which waited for: 2 -> 2; matrix products, arithmetic and copies ran while one was open for 11% -> 7% of each run, Pallas kernels for 0% -> 0%
where the time goes in v1:
time: 58.8 us; the launch traced here: 57.7 us
  local copies, waits for them, and re-layouts  23.2 us (39%)
  starting transfers between devices  11.9 us (20%)
  waiting for transfers between devices  8.62 us (15%)
  matrix products  8.4 us (14%)
  other arithmetic  4.87 us (8%)
  between operations  0.72 us (1%)
    unnamed x15, local copies, waits for them, and re-layouts  19.9 us
    all_to_all x1, starting transfers between devices, shards(): lax.all_to_all(jnp.stack(jnp.split(snapshots, lax.axis_size('space'), axi...  7.39 us
    all_to_all x1, waiting for transfers between devices, shards(): lax.all_to_all(jnp.stack(jnp.split(snapshots, lax.axis_size('space'), axi...  6.06 us
    dot_general x1, matrix products, add_grad(): jnp.einsum('tgo,tgc->goc', resid, inputs, preferred_element_type=jnp.floa...  5.49 us
    ppermute x1, starting transfers between devices, extended(): after = lax.ppermute(initial, axis, down)  4.43 us
    sort x1, other arithmetic, shards(): order = jnp.argsort(time_of)  3.19 us
    dot_general x1, matrix products, add_error(): jnp.einsum('tgc,goc->tgo', inputs, new_rounded, preferred_element_type=jn...  2.91 us
    ppermute x1, waiting for transfers between devices, extended(): before = lax.ppermute(last, axis, up)  2.55 us
  transfers between devices with their start and end apart: 3, of which 2 were waited for; matrix products, arithmetic and copies ran while one was open for 7% of the time, Pallas kernels for 0%

profile of v1, /device:TPU:0, one launch (start us, length us, event | category | flops | bytes accessed | tf_op | source)
XLA Modules:
  0.0 57.7 jit_solution(5357058615090368308)
XLA Ops:
  0.6 1.3 %constant_dynamic-update-slice_fusion.15 = bf16[16,8,8,128]{3,2,1,0:T(8,128)(2,1)} fusion(bf16[8,128,128]{2,1,0:T(8,128)(2,1)} %param.4), kind=kLoop, calls=%fused_computation.43 | loop fusion | bytes 32768
  2.0 1.3 %constant_dynamic-update-slice_fusion.14 = bf16[16,8,8,128]{3,2,1,0:T(8,128)(2,1)} fusion(bf16[16,8,8,128]{3,2,1,0:T(8,128)(2,1)} %constant_dynamic-update-slice_fusion.15, bf16[8,128,128]{2,1,0:T(8,128)(2,1)} %param.4), kind=kLoop, calls=%fused_computation.42 | loop fusion | bytes 32768
  3.3 1.3 %constant_dynamic-update-slice_fusion.13 = bf16[16,8,8,128]{3,2,1,0:T(8,128)(2,1)} fusion(bf16[16,8,8,128]{3,2,1,0:T(8,128)(2,1)} %constant_dynamic-update-slice_fusion.14, bf16[8,128,128]{2,1,0:T(8,128)(2,1)} %param.4), kind=kLoop, calls=%fused_computation.41 | loop fusion | bytes 32768
  4.6 1.3 %constant_dynamic-update-slice_fusion.12 = bf16[16,8,8,128]{3,2,1,0:T(8,128)(2,1)} fusion(bf16[16,8,8,128]{3,2,1,0:T(8,128)(2,1)} %constant_dynamic-update-slice_fusion.13, bf16[8,128,128]{2,1,0:T(8,128)(2,1)} %param.4), kind=kLoop, calls=%fused_computation.40 | loop fusion | bytes 32768
  5.9 1.3 %constant_dynamic-update-slice_fusion.11 = bf16[16,8,8,128]{3,2,1,0:T(8,128)(2,1)} fusion(bf16[16,8,8,128]{3,2,1,0:T(8,128)(2,1)} %constant_dynamic-update-slice_fusion.12, bf16[8,128,128]{2,1,0:T(8,128)(2,1)} %param.4), kind=kLoop, calls=%fused_computation.39 | loop fusion | bytes 32768
  7.2 1.3 %constant_dynamic-update-slice_fusion.10 = bf16[16,8,8,128]{3,2,1,0:T(8,128)(2,1)} fusion(bf16[16,8,8,128]{3,2,1,0:T(8,128)(2,1)} %constant_dynamic-update-slice_fusion.11, bf16[8,128,128]{2,1,0:T(8,128)(2,1)} %param.4), kind=kLoop, calls=%fused_computation.38 | loop fusion | bytes 32768
  8.6 1.3 %constant_dynamic-update-slice_fusion.9 = bf16[16,8,8,128]{3,2,1,0:T(8,128)(2,1)} fusion(bf16[16,8,8,128]{3,2,1,0:T(8,128)(2,1)} %constant_dynamic-update-slice_fusion.10, bf16[8,128,128]{2,1,0:T(8,128)(2,1)} %param.4), kind=kLoop, calls=%fused_computation.37 | loop fusion | bytes 32768
  9.9 1.3 %constant_dynamic-update-slice_fusion.8 = bf16[16,8,8,128]{3,2,1,0:T(8,128)(2,1)} fusion(bf16[16,8,8,128]{3,2,1,0:T(8,128)(2,1)} %constant_dynamic-update-slice_fusion.9, bf16[8,128,128]{2,1,0:T(8,128)(2,1)} %param.4), kind=kLoop, calls=%fused_computation.36 | loop fusion | bytes 32768
  11.2 1.3 %constant_dynamic-update-slice_fusion.7 = bf16[16,8,8,128]{3,2,1,0:T(8,128)(2,1)} fusion(bf16[16,8,8,128]{3,2,1,0:T(8,128)(2,1)} %constant_dynamic-update-slice_fusion.8, bf16[8,128,128]{2,1,0:T(8,128)(2,1)} %param.4), kind=kLoop, calls=%fused_computation.35 | loop fusion | bytes 32768
  12.5 1.3 %constant_dynamic-update-slice_fusion.6 = bf16[16,8,8,128]{3,2,1,0:T(8,128)(2,1)} fusion(bf16[16,8,8,128]{3,2,1,0:T(8,128)(2,1)} %constant_dynamic-update-slice_fusion.7, bf16[8,128,128]{2,1,0:T(8,128)(2,1)} %param.4), kind=kLoop, calls=%fused_computation.34 | loop fusion | bytes 32768
  13.9 1.3 %constant_dynamic-update-slice_fusion.5 = bf16[16,8,8,128]{3,2,1,0:T(8,128)(2,1)} fusion(bf16[16,8,8,128]{3,2,1,0:T(8,128)(2,1)} %constant_dynamic-update-slice_fusion.6, bf16[8,128,128]{2,1,0:T(8,128)(2,1)} %param.4), kind=kLoop, calls=%fused_computation.33 | loop fusion | bytes 32768
  15.2 1.3 %constant_dynamic-update-slice_fusion.4 = bf16[16,8,8,128]{3,2,1,0:T(8,128)(2,1)} fusion(bf16[16,8,8,128]{3,2,1,0:T(8,128)(2,1)} %constant_dynamic-update-slice_fusion.5, bf16[8,128,128]{2,1,0:T(8,128)(2,1)} %param.4), kind=kLoop, calls=%fused_computation.32 | loop fusion | bytes 32768
  16.5 1.3 %constant_dynamic-update-slice_fusion.3 = bf16[16,8,8,128]{3,2,1,0:T(8,128)(2,1)} fusion(bf16[16,8,8,128]{3,2,1,0:T(8,128)(2,1)} %constant_dynamic-update-slice_fusion.4, bf16[8,128,128]{2,1,0:T(8,128)(2,1)} %param.4), kind=kLoop, calls=%fused_computation.31 | loop fusion | bytes 32768
  17.8 1.3 %constant_dynamic-update-slice_fusion.2 = bf16[16,8,8,128]{3,2,1,0:T(8,128)(2,1)} fusion(bf16[16,8,8,128]{3,2,1,0:T(8,128)(2,1)} %constant_dynamic-update-slice_fusion.3, bf16[8,128,128]{2,1,0:T(8,128)(2,1)} %param.4), kind=kLoop, calls=%fused_computation.30 | loop fusion | bytes 32768
  19.2 1.3 %constant_dynamic-update-slice_fusion.1 = bf16[16,8,8,128]{3,2,1,0:T(8,128)(2,1)} fusion(bf16[16,8,8,128]{3,2,1,0:T(8,128)(2,1)} %constant_dynamic-update-slice_fusion.2, bf16[8,128,128]{2,1,0:T(8,128)(2,1)} %param.4), kind=kLoop, calls=%fused_computation.29 | loop fusion | bytes 32768
  20.5 1.3 %constant_dynamic-update-slice_fusion = bf16[16,8,8,128]{3,2,1,0:T(8,128)(2,1)} fusion(bf16[16,8,8,128]{3,2,1,0:T(8,128)(2,1)} %constant_dynamic-update-slice_fusion.1, bf16[8,128,128]{2,1,0:T(8,128)(2,1)} %param.4), kind=kLoop, calls=%fused_computation.28 | loop fusion | bytes 32768 | tf_op jit(solution)/shard_map/stack | solution.py:31
  21.8 7.4 %all-to-all-start = ((bf16[16,8,8,128]{3,2,1,0:T(8,128)(2,1)}), bf16[16,8,8,128]{3,2,1,0:T(8,128)(2,1)S(1)}, u32[]{:S(2)}, u32[]{:S(2)}) async-start(bf16[16,8,8,128]{3,2,1,0:T(8,128)(2,1)} %constant_dynamic-update-slice_fusion), calls=%async_computation | async-start | bytes 524288 | tf_op jit(solution)/shard_map/all_to_all | solution.py:30
  29.2 3.2 %sort.17 = (s32[128]{0:T(128)}, s32[128]{0:T(128)S(1)}) sort(s32[128]{0:T(128)} %param.7, s32[128]{0:T(128)S(1)} %iota.22), dimensions={0}, to_apply=%region_0.0 | sort | flops 896 | bytes 2048 | tf_op jit(solution)/shard_map/jit(argsort)/sort | solution.py:36
  32.4 0.8 %compare_select_fusion = s32[8,8]{1,0:T(8,128)S(1)} fusion(s32[8,8]{1,0:T(8,128)} %param.6, s32[8]{0:T(128)S(1)} %iota_add_fusion), kind=kLoop, calls=%fused_computation.44 | loop fusion | flops 1088 | bytes 544 | tf_op jit(solution)/shard_map/while/body/eval_jaxpr/select_n | solution.py:50
  33.2 6.1 %all-to-all-done = bf16[16,8,8,128]{3,2,1,0:T(8,128)(2,1)S(1)} async-done(((bf16[16,8,8,128]{3,2,1,0:T(8,128)(2,1)}), bf16[16,8,8,128]{3,2,1,0:T(8,128)(2,1)S(1)}, u32[]{:S(2)}, u32[]{:S(2)}) %all-to-all-start) | async-done | bytes 262176 | tf_op jit(solution)/shard_map/all_to_all | solution.py:30
  39.2 0.1 fusion.63
  39.3 0.1 collective-permute-start
  39.4 4.4 %collective-permute-start.1 = (bf16[128,4,128]{2,1,0:T(4,128)(2,1)S(1)}, bf16[128,4,128]{2,1,0:T(4,128)(2,1)S(1)}, u32[]{:S(2)}, u32[]{:S(2)}) collective-permute-start(bf16[128,4,128]{2,1,0:T(4,128)(2,1)S(1)} %get-tuple-element.33), channel_id=1, source_target_pairs={{1,0},{2,1},{3,2},{4,3},{5,4},{6,5},{7,6},{8,7},{9,8},{10,9},{11,1... | collective-permute-start | bytes 393224 | tf_op jit(solution)/shard_map/ppermute | solution.py:17
  43.8 0.1 reshape.34
  43.9 2.6 %collective-permute-done = bf16[128,4,128]{2,1,0:T(4,128)(2,1)S(1)} collective-permute-done((bf16[128,4,128]{2,1,0:T(4,128)(2,1)S(1)}, bf16[128,4,128]{2,1,0:T(4,128)(2,1)S(1)}, u32[]{:S(2)}, u32[]{:S(2)}) %collective-permute-start) | collective-permute-done | bytes 131104 | tf_op jit(solution)/shard_map/ppermute | solution.py:16
  46.5 0.0 collective-permute-done.1
  46.5 0.3 pad_maximum_fusion
  46.8 0.7 %gather_fusion = bf16[128,16,128]{2,1,0:T(8,128)(2,1)S(1)} fusion(bf16[128,16,128]{2,1,0:T(8,128)(2,1)S(1)} %pad_maximum_fusion, s32[1024]{0:T(1024)S(1)} %pad_clamp_fusion.1), kind=kCustom, calls=%fused_computation | custom fusion | bytes 1049088 | tf_op jit(solution)/shard_map/gather | solution.py:37
  47.5 0.1 copy.14
  47.7 0.1 slice.27
  47.7 1.0 %gather_fusion.1 = bf16[64,128,128]{2,1,0:T(8,128)(2,1)S(1)} fusion(bf16[128,16,128]{2,0,1:T(8,128)(2,1)S(1)} %copy.14, s32[1024]{0:T(1024)S(1)} %pad_clamp_fusion), kind=kCustom, calls=%fused_computation.1 | custom fusion | bytes 4194560 | tf_op jit(solution)/shard_map/while/body/eval_jaxpr/gather | solution.py:50
  48.7 5.5 %multiply_subtract_fusion = f32[8,128,1024]{2,1,0:T(8,128)} fusion(bf16[8,128,1024]{2,1,0:T(8,128)(2,1)} %param.5, bf16[8,8,16,8,128]{4,3,2,1,0:T(8,128)(2,1)S(1)} %bitcast.89, f32[128]{0:T(128)S(1)} %compare_convert_fusion, bf16[1,8,128]{2,0,1:T(2,128)(2,1)S(1)} %slice.28, bf16[127,8,128]{2,0,1:T(8,128)(2,1)S(1)} %slice.27), kind=kOutput, calls=%fused_computation.2 | convolution fusion | flops 541065216 | bytes 8651264 | tf_op jit(solution)/shard_map/while/body/eval_jaxpr/tgo,tgc->goc/dot_general | solution.py:62
  54.2 2.9 %fusion.51 = f32[8,128]{1,0:T(8,128)S(1)} fusion(bf16[8,8,16,8,128]{4,3,2,1,0:T(8,128)(2,1)S(1)} %bitcast.90, f32[8,128,1024]{2,1,0:T(8,128)} %multiply_subtract_fusion, f32[128]{0:T(128)S(1)} %compare_convert_fusion, bf16[1,8,128]{2,0,1:T(2,128)(2,1)S(1)} %slice.28, bf16[127,8,128]{2,0,1:T(8,128)(2,1)S(1)} %slice.27), kind=kOutput, calls=%fused_computation.22 | convolution fusion | flops 270662656 | bytes 6558208 | tf_op jit(solution)/shard_map/while/body/eval_jaxpr/tgc,goc->tgo/dot_general | solution.py:71
  57.1 0.6 %broadcast_multiply_fusion = f32[8,128]{1,0:T(8,128)} fusion(f32[8,128]{1,0:T(8,128)S(1)} %fusion.51), kind=kLoop, calls=%fused_computation.53 | loop fusion | flops 1024 | bytes 8192 | tf_op jit(solution)/shard_map/div | solution.py:78
  (7 shorter events, 0.0 us)
Async XLA Ops:
  21.8 17.4 %all-to-all-start = ((bf16[16,8,8,128]{3,2,1,0:T(8,128)(2,1)}), bf16[16,8,8,128]{3,2,1,0:T(8,128)(2,1)S(1)}, u32[]{:S(2)}, u32[]{:S(2)}) async-start(bf16[16,8,8,128]{3,2,1,0:T(8,128)(2,1)} %constant_dynamic-update-slice_fusion), calls=%async_computation | async-start | bytes 524288 | tf_op jit(solution)/shard_map/all_to_all | solution.py:30
  39.3 7.1 %collective-permute-start = (bf16[128,4,128]{2,1,0:T(4,128)(2,1)S(1)}, bf16[128,4,128]{2,1,0:T(4,128)(2,1)S(1)}, u32[]{:S(2)}, u32[]{:S(2)}) collective-permute-start(bf16[128,4,128]{2,1,0:T(4,128)(2,1)S(1)} %get-tuple-element.32), channel_id=1, source_target_pairs={{0,1},{1,2},{2,3},{3,4},{4,5},{5,6},{6,7},{7,8},{8,9},{9,10},{10,1... | collective-permute-start | bytes 393224 | tf_op jit(solution)/shard_map/ppermute | solution.py:16
  39.4 7.1 %collective-permute-start.1 = (bf16[128,4,128]{2,1,0:T(4,128)(2,1)S(1)}, bf16[128,4,128]{2,1,0:T(4,128)(2,1)S(1)}, u32[]{:S(2)}, u32[]{:S(2)}) collective-permute-start(bf16[128,4,128]{2,1,0:T(4,128)(2,1)S(1)} %get-tuple-element.33), channel_id=1, source_target_pairs={{1,0},{2,1},{3,2},{4,3},{5,4},{6,5},{7,6},{8,7},{9,8},{10,9},{11,1... | collective-permute-start | bytes 393224 | tf_op jit(solution)/shard_map/ppermute | solution.py:17
